TPU v7x, 32 devices: a whole 2x2x4 slice. The times are simulated.
32 devices in a mesh: phase: 2 (over x), seq: 16 (over z, y, core).
Axes of the slice: x: 2, y: 2, z: 4, core: 2. Of those that a mesh axis runs over, the one named last changes fastest.
Arguments:
- tokens: bfloat16 [1024, 1024], P('seq'), may hold values from -6 to 6
- phase_weight: bfloat16 [2, 1024, 1024], P('phase'), may hold values from -0.1875 to 0.1875
- phase_gain: float32 [2, 1024], P('phase'), may hold values from 0.25 to 1.75
- unit_weight: bfloat16 [1024, 1024], replicated, may hold values from -0.1875 to 0.1875
- unit_gain: float32 [1024], replicated, may hold values from 0.25 to 1.75
- durations: int32 [1024], P('seq'), may hold values from 4 to 32, as said below
Outputs:
- encoder_out: bfloat16 [1024, 1024], P('seq')
- unit_states: bfloat16 [8192, 1024], P(('phase', 'seq'))
Inputs may be any that keep to these rules, and one draw needn't show every extreme that they name: durations sum to 8192; some token has exactly 32 frames and some exactly 4.
All inputs are finite; a program needn't handle non-finite values.
Results may differ from a plain program's by a relative error of at most 0.0062.
Values may be sent and summed in bfloat16 or wider, within the bound.
A program may use at most 64 MiB of HBM per device.

v0:
```python
import jax
import jax.numpy as jnp
from jax import lax
from jax.sharding import PartitionSpec as P

FR_DEV = 256


def from_behind(block, axis, distance):
    devices = range(lax.axis_size(axis))
    route = [(i - distance, i) for i in devices if i - distance in devices]
    return lax.ppermute(block, axis, route)


def from_root(array, axis, root):
    mine = lax.axis_index(axis) == root
    return lax.psum(jnp.where(mine, array, jnp.zeros_like(array)), axis)


def carried_in(array, axis, combine, identity):
    peers, mine = (lax.axis_size(axis), lax.axis_index(axis))
    everything = lax.all_gather(array, axis)
    start = jnp.broadcast_to(jnp.asarray(identity, array.dtype), array.shape)

    def turn(k, before):
        reached = k < mine
        new = combine(before, everything[k])
        return jnp.where(reached, new, before)

    return lax.fori_loop(0, peers, turn, start)


def layer(values_in, weight, gain):
    widened = values_in.astype(jnp.float32)
    scaled = widened * gain / jnp.sqrt(jnp.mean(widened * widened, axis=-1, keepdims=True) + 1e-06)
    normed = scaled.astype(jnp.bfloat16)
    branch = jax.nn.silu(jnp.dot(normed, weight, preferred_element_type=jnp.float32))
    return (widened + branch).astype(jnp.bfloat16)


def shards(tokens, phase_weight, phase_gain, unit_weight, unit_gain, durations):
    weight = phase_weight[0]
    gain_row = phase_gain[0]
    phases = lax.axis_size("phase")
    seqsize = lax.axis_size("seq")
    phase_index = lax.axis_index("phase")

    def whole_step(turn_index, current):
        return from_behind(layer(current, weight, gain_row), "phase", 1)

    hidden = layer(lax.fori_loop(0, phases - 1, whole_step, tokens), weight, gain_row)
    hidden = from_root(hidden, "phase", phases - 1)
    offset = carried_in(
        jnp.sum(durations), "seq", lambda earlier, latest: earlier + latest, jnp.int32(0)
    )
    frame_ends = offset + jnp.cumsum(durations)
    begins = frame_ends - durations
    first_frame = (phase_index * seqsize + lax.axis_index("seq")) * FR_DEV
    frames = first_frame + lax.iota(jnp.int32, FR_DEV)
    tok_count = durations.shape[0]
    min_frames = max(phases * FR_DEV // (2 * tok_count), 1)
    slot_count = min(tok_count, (FR_DEV - 2) // min_frames + 2)
    frame_low = (phase_index * seqsize + lax.iota(jnp.int32, seqsize)) * FR_DEV
    frame_high = frame_low + FR_DEV
    firsts = jnp.sum((frame_ends[None, :] <= frame_low[:, None]).astype(jnp.int32), axis=1)
    wanted = (firsts[:, None] + lax.iota(jnp.int32, slot_count)[None, :]).reshape(-1)
    clamped = jnp.minimum(wanted, tok_count - 1)
    usable = (wanted < tok_count) & (begins[clamped] < jnp.repeat(frame_high, slot_count))
    send_rows = jnp.where(usable[:, None], hidden[clamped], jnp.zeros((), jnp.bfloat16))
    send_begin = jnp.where(usable, begins[clamped], 0).astype(jnp.int32)
    send_end = jnp.where(usable, frame_ends[clamped], 0).astype(jnp.int32)
    got_rows, got_begin, got_end = (
        lax.all_to_all(send_rows, "seq", split_axis=0, concat_axis=0, tiled=True),
        lax.all_to_all(send_begin, "seq", split_axis=0, concat_axis=0, tiled=True),
        lax.all_to_all(send_end, "seq", split_axis=0, concat_axis=0, tiled=True),
    )
    member = (frames[:, None] >= got_begin[None, :]) & (frames[:, None] < got_end[None, :])
    expanded = jnp.dot(
        member.astype(jnp.bfloat16), got_rows, preferred_element_type=jnp.float32
    ).astype(jnp.bfloat16)
    unit_states = layer(expanded, unit_weight, unit_gain)
    return (hidden, unit_states)


def solution(mesh):
    return jax.shard_map(
        shards,
        mesh=mesh,
        in_specs=(P("seq", None), P("phase", None, None), P("phase", None), P(), P(), P("seq")),
        out_specs=(P("seq", None), P(("phase", "seq"), None)),
        check_vma=False,
    )
```

profile of v0, /device:TPU:13, one launch (start us, length us, event | category | flops | bytes accessed | tf_op | source)
XLA Modules:
  0.0 257.4 jit_solution(7181134546518761841)
XLA Ops:
  7.2 1.5 reduce_sum.48
  8.7 1.2 dynamic-slice
  9.9 1.4 dynamic-update-slice
  11.3 7.9 %all-reduce = s32[16]{0:T(128)S(1)} all-reduce(s32[16]{0:T(128)S(1)} %dynamic-update-slice), channel_id=1, replica_groups=mesh['phase'=2,'seq'=16] {'seq'}, use_global_device_ids=true, to_apply=%add | all-reduce | flops 16 | bytes 128
  19.2 22.2 %while.8 = (s32[]{:T(128)}, s32[]{:T(128)}, s32[]{:T(128)}, s32[16]{0:T(128)S(1)}, s32[]{:T(128)}) while((s32[]{:T(128)}, s32[]{:T(128)}, s32[]{:T(128)}, s32[16]{0:T(128)S(1)}, s32[]{:T(128)}) %tuple.221), condition=%wide.region_5.6_spmd, body=%wide.region_4.5_spmd.sunk | while | flops 5 | bytes 115 | solution.py:30
  20.6 0.7 dynamic_slice.8
  22.0 0.7 dynamic_slice.8
  41.4 0.7 copy.13
  42.4 0.7 sub.3
  43.0 0.7 fusion.55
  43.7 0.7 fusion.53
  44.4 0.7 fusion.52
  45.2 0.7 fusion.54
  48.9 40.1 %select_select_fusion = (s32[1024]{0:T(1024)S(1)}, pred[1024]{0:T(1024)(128)(4,1)S(1)}, pred[1024]{0:T(1024)(128)(4,1)S(1)}, pred[1024]{0:T(1024)(128)(4,1)S(1)}...) fusion(s32[]{:T(128)} %bitcast.72, s32[]{:T(128)} %bitcast.73, ...), kind=kLoop, calls=%fused_computation.53 | loop fusion | flops 129024 | bytes 72960 | tf_op jit(solution)/shard_map/gather | solution.py:71
  89.0 40.0 %select_select_fusion.1 = s32[1024]{0:T(1024)S(1)} fusion(pred[1024]{0:T(1024)(128)(4,1)S(1)} %get-tuple-element.165, pred[1024]{0:T(1024)(128)(4,1)S(1)} %get-tuple-element.164, pred[1024]{0:T(1024)(128)(4,1)S(1)} %get-tuple-element.163, pred[1024]{0:T(1024)(128)(4,1)S(1)} %get-tuple-element.162, pred[1024]{0:T(1024)(128)(4,1)S(1)} %get-tuple-element.161, ...), kind=kLoop, calls=%fused_computation.54 | loop fusion | flops 64512 | bytes 68864 | tf_op jit(solution)/shard_map/gather | solution.py:68
  129.1 0.7 fusion.46
  129.7 8.4 %all-to-all-start.1 = ((s32[16,64,1]{1,2,0:T(1,128)}), s32[16,64,1]{1,2,0:T(1,128)S(1)}, u32[]{:S(2)}, u32[]{:S(2)}) async-start(s32[16,64,1]{1,2,0:T(1,128)} %bitcast.136), calls=%async_computation.1 | async-start | bytes 16384 | tf_op jit(solution)/shard_map/all_to_all | solution.py:75
  138.2 1.0 fusion.22
  139.3 2.3 fusion.23
  141.5 3.1 %collective-permute-start = (bf16[64,1024]{1,0:T(8,128)(2,1)S(1)}, bf16[64,1024]{1,0:T(8,128)(2,1)S(1)}, u32[]{:S(2)}, u32[]{:S(2)}) collective-permute-start(bf16[64,1024]{1,0:T(8,128)(2,1)S(1)} %fusion.23), channel_id=1, source_target_pairs={{0,16},{1,17},{2,18},{3,19},{4,20},{5,21},{6,22},{7,23},{8,24},{9,... | collective-permute-start | bytes 393224 | tf_op jit(solution)/shard_map/while/body/eval_jaxpr/ppermute | solution.py:12
  144.8 2.3 collective-permute-done
  147.3 2.8 %fusion.30 = bf16[64,1024]{1,0:T(8,128)(2,1)} fusion(bf16[1,1024,1024]{2,1,0:T(8,128)(2,1)} %param.9, bf16[64,1024]{1,0:T(8,128)(2,1)S(1)} %collective-permute-done, f32[64]{0:T(128)S(1)} %add_sqrt_fusion.1, f32[1024]{0:T(1024)S(1)} %bitcast.160, pred[]{:T(512)S(6)} %eq.3), kind=kOutput, calls=%fused_computation.37 | convolution fusion | flops 135004160 | bytes 2363649 | tf_op jit(solution)/shard_map/dot_general | solution.py:37
  150.2 23.6 %all-reduce.3.cloned.1.call-done = bf16[64,1024]{1,0:T(8,128)(2,1)} async-done(((bf16[64,1024]{1,0:T(8,128)(2,1)}), bf16[64,1024]{1,0:T(8,128)(2,1)}) %all-reduce.3.cloned.1.call-update) | async-done | bytes 131088 | tf_op jit(solution)/shard_map/psum | solution.py:17
  173.7 7.0 %gather_fusion = bf16[1024,1024]{1,0:T(8,128)(2,1)} fusion(bf16[64,1024]{1,0:T(8,128)(2,1)} %all-reduce.3.cloned.1.call-done, s32[1024]{0:T(1024)S(1)} %broadcast_clamp_fusion), kind=kCustom, calls=%fused_computation | custom fusion | bytes 4198400 | tf_op jit(solution)/shard_map/gather | solution.py:69
  180.7 6.8 %all-to-all-start = ((s32[16,64,1]{1,2,0:T(1,128)}), s32[16,64,1]{1,2,0:T(1,128)S(1)}, u32[]{:S(2)}, u32[]{:S(2)}) async-start(s32[16,64,1]{1,2,0:T(1,128)} %bitcast.71), calls=%async_computation | async-start | bytes 16384 | tf_op jit(solution)/shard_map/all_to_all | solution.py:74
  187.5 3.2 %broadcast_select_fusion = bf16[16,64,1024]{2,1,0:T(8,128)(2,1)} fusion(bf16[16,64,1024]{2,1,0:T(8,128)(2,1)} %bitcast.155, pred[16,64]{1,0:T(8,128)(4,1)S(1)} %fusion.44), kind=kLoop, calls=%fused_computation.5 | loop fusion | flops 1048576 | bytes 4195328 | tf_op jit(solution)/shard_map/jit(_where)/select_n | solution.py:69
  191.3 6.9 %all-to-all-start.2 = ((bf16[16,64,1024]{2,1,0:T(8,128)(2,1)}), bf16[16,64,1024]{2,1,0:T(8,128)(2,1)}, u32[]{:S(2)}, u32[]{:S(2)}) async-start(bf16[16,64,1024]{2,1,0:T(8,128)(2,1)} %broadcast_select_fusion), calls=%async_computation.2 | async-start | bytes 4194304 | tf_op jit(solution)/shard_map/all_to_all | solution.py:73
  198.7 0.7 reduce.7
  199.5 0.7 reduce.8
  200.2 45.5 %all-to-all-done.2 = bf16[16,64,1024]{2,1,0:T(8,128)(2,1)} async-done(((bf16[16,64,1024]{2,1,0:T(8,128)(2,1)}), bf16[16,64,1024]{2,1,0:T(8,128)(2,1)}, u32[]{:S(2)}, u32[]{:S(2)}) %all-to-all-start.2) | async-done | bytes 2097184 | tf_op jit(solution)/shard_map/all_to_all | solution.py:73
  245.7 2.4 fusion.6
  248.2 1.7 fusion.7
  (52 shorter events, 14.9 us)
Async XLA Ops:
  7.2 241.0 %copy-start = (bf16[1024,1024]{1,0:T(8,128)(2,1)S(1)}, bf16[1024,1024]{1,0:T(8,128)(2,1)}, u32[]{:S(2)}) copy-start(bf16[1024,1024]{1,0:T(8,128)(2,1)} %param.11) | copy-start | bytes 6291460
  89.0 58.3 %copy-start.2 = (f32[1,1024]{1,0:T(1,128)S(1)}, f32[1,1024]{1,0:T(1,128)}, u32[]{:S(2)}) copy-start(f32[1,1024]{1,0:T(1,128)} %param.10) | copy-start | bytes 12292
  129.7 51.0 %all-to-all-start.1 = ((s32[16,64,1]{1,2,0:T(1,128)}), s32[16,64,1]{1,2,0:T(1,128)S(1)}, u32[]{:S(2)}, u32[]{:S(2)}) async-start(s32[16,64,1]{1,2,0:T(1,128)} %bitcast.136), calls=%async_computation.1 | async-start | bytes 16384 | tf_op jit(solution)/shard_map/all_to_all | solution.py:75
  138.2 35.6 %all-reduce.3.cloned.1.call-start = ((), (), s32[]{:S(2)}) async-start(), calls=%async_computation.3 | async-start | bytes 262144 | tf_op jit(solution)/shard_map/psum | solution.py:17
  141.5 5.6 %collective-permute-start = (bf16[64,1024]{1,0:T(8,128)(2,1)S(1)}, bf16[64,1024]{1,0:T(8,128)(2,1)S(1)}, u32[]{:S(2)}, u32[]{:S(2)}) collective-permute-start(bf16[64,1024]{1,0:T(8,128)(2,1)S(1)} %fusion.23), channel_id=1, source_target_pairs={{0,16},{1,17},{2,18},{3,19},{4,20},{5,21},{6,22},{7,23},{8,24},{9,... | collective-permute-start | bytes 393224 | tf_op jit(solution)/shard_map/while/body/eval_jaxpr/ppermute | solution.py:12
  180.7 10.5 %all-to-all-start = ((s32[16,64,1]{1,2,0:T(1,128)}), s32[16,64,1]{1,2,0:T(1,128)S(1)}, u32[]{:S(2)}, u32[]{:S(2)}) async-start(s32[16,64,1]{1,2,0:T(1,128)} %bitcast.71), calls=%async_computation | async-start | bytes 16384 | tf_op jit(solution)/shard_map/all_to_all | solution.py:74
  191.3 54.4 %all-to-all-start.2 = ((bf16[16,64,1024]{2,1,0:T(8,128)(2,1)}), bf16[16,64,1024]{2,1,0:T(8,128)(2,1)}, u32[]{:S(2)}, u32[]{:S(2)}) async-start(bf16[16,64,1024]{2,1,0:T(8,128)(2,1)} %broadcast_select_fusion), calls=%async_computation.2 | async-start | bytes 4194304 | tf_op jit(solution)/shard_map/all_to_all | solution.py:73
  198.7 49.5 %copy-start.3 = (f32[1024]{0:T(1024)S(1)}, f32[1024]{0:T(1024)}, u32[]{:S(2)}) copy-start(f32[1024]{0:T(1024)} %param.12) | copy-start | bytes 12292
  248.2 1.7 copy-start.1
Sparse Core Ops, SparseCore 0:
  150.3 23.4 all-reduce.2
where the time goes:
time: 259 us; the launch traced here: 257 us
  other arithmetic  89.2 us (34%)
  waiting for transfers between devices  72 us (28%)
  local copies, waits for them, and re-layouts  28 us (11%)
  starting transfers between devices  25.3 us (10%)
  between operations  14.2 us (5%)
  loops' own time  11.6 us (4%)
  matrix products  9.25 us (4%)
  blocking collectives  7.88 us (3%)
    all_to_all x1, waiting for transfers between devices, shards(): lax.all_to_all(send_rows, 'seq', split_axis=0, concat_axis=0, tiled=True)  45.5 us
    gather x1, other arithmetic, shards(): send_end = jnp.where(usable, frame_ends[clamped], 0).astype(jnp.int32)  40.1 us
    gather x1, other arithmetic, shards(): begins[clamped] < jnp.repeat(frame_high, slot_count)  40 us
    psum x1, waiting for transfers between devices, from_root(): return lax.psum(jnp.where(mine, array, jnp.zeros_like(array)), axis)  23.6 us
    another operation x1, loops' own time, carried_in(): return lax.fori_loop(0, peers, turn, start)  11.6 us
    dynamic_slice x16, local copies, waits for them, and re-layouts, turn(): new = combine(before, everything[k])  10.7 us
    all_to_all x1, starting transfers between devices, shards(): lax.all_to_all(send_end, 'seq', split_axis=0, concat_axis=0, tiled=True)  8.42 us
    unnamed x1, blocking collectives  7.88 us
  transfers between devices with their start and end apart: 5, of which 4 were waited for; matrix products, arithmetic and copies ran while one was open for 7% of the time, Pallas kernels for 0%

commit v1 on v0

--- a/solution.py
+++ b/solution.py
@@ -14,7 +14,7 @@
 
 def from_root(array, axis, root):
     mine = lax.axis_index(axis) == root
-    return lax.psum(jnp.where(mine, array, jnp.zeros_like(array)), axis)
+    return jnp.sum(lax.all_gather(jnp.where(mine, array, jnp.zeros_like(array)), axis), axis=0)
 
 
 def carried_in(array, axis, combine, identity):

time: 259 us -> 226 us (0.87)
  waiting for transfers between devices: 72 us -> 48.4 us
  between operations: 14.2 us -> 0.8 us
  blocking collectives: 7.88 us -> 13.1 us
    psum x1 -> x0, waiting for transfers between devices: 23.6 us -> none  [from_root(): return lax.psum(jnp.where(mine, array, jnp.zeros_like(array)), axis)]
    all_gather x0 -> x1, blocking collectives: none -> 5.22 us  [from_root(): lax.all_gather(jnp.where(mine, array, jnp.zeros_like(array)), axis)]
  transfers between devices with their start and end apart: 5 -> 4, of which waited for: 4 -> 3; matrix products, arithmetic and copies ran while one was open for 7% -> 7% of each run, Pallas kernels for 0% -> 0%
where the time goes in v1:
time: 226 us; the launch traced here: 224 us
  other arithmetic  89.2 us (39%)
  waiting for transfers between devices  48.4 us (21%)
  starting transfers between devices  26.2 us (12%)
  local copies, waits for them, and re-layouts  25.8 us (11%)
  blocking collectives  13.1 us (6%)
  loops' own time  11.6 us (5%)
  matrix products  8.59 us (4%)
    all_to_all x1, waiting for transfers between devices, shards(): lax.all_to_all(send_rows, 'seq', split_axis=0, concat_axis=0, tiled=True)  45.5 us
    gather x1, other arithmetic, shards(): send_end = jnp.where(usable, frame_ends[clamped], 0).astype(jnp.int32)  40.1 us
    gather x1, other arithmetic, shards(): begins[clamped] < jnp.repeat(frame_high, slot_count)  40 us
    another operation x1, loops' own time, carried_in(): return lax.fori_loop(0, peers, turn, start)  11.6 us
    dynamic_slice x16, local copies, waits for them, and re-layouts, turn(): new = combine(before, everything[k])  10.7 us
    all_to_all x1, starting transfers between devices, shards(): lax.all_to_all(send_end, 'seq', split_axis=0, concat_axis=0, tiled=True)  8.42 us
    unnamed x1, blocking collectives  7.88 us
    all_to_all x1, starting transfers between devices, shards(): lax.all_to_all(send_begin, 'seq', split_axis=0, concat_axis=0, tiled=True)  7.8 us
  transfers between devices with their start and end apart: 4, of which 3 were waited for; matrix products, arithmetic and copies ran while one was open for 7% of the time, Pallas kernels for 0%

profile of v1, /device:TPU:13, one launch (start us, length us, event | category | flops | bytes accessed | tf_op | source)
XLA Modules:
  0.0 223.7 jit_solution(5975949263409341543)
XLA Ops:
  0.6 1.5 reduce_sum.61
  2.2 1.2 dynamic-slice
  3.4 1.4 dynamic-update-slice
  4.8 7.9 %all-reduce = s32[16]{0:T(128)S(1)} all-reduce(s32[16]{0:T(128)S(1)} %dynamic-update-slice), channel_id=1, replica_groups=mesh['phase'=2,'seq'=16] {'seq'}, use_global_device_ids=true, to_apply=%add | all-reduce | flops 16 | bytes 128
  12.6 22.2 %while.8 = (s32[]{:T(128)}, s32[]{:T(128)}, s32[]{:T(128)}, s32[16]{0:T(128)S(1)}, s32[]{:T(128)}) while((s32[]{:T(128)}, s32[]{:T(128)}, s32[]{:T(128)}, s32[16]{0:T(128)S(1)}, s32[]{:T(128)}) %tuple.221), condition=%wide.region_5.6_spmd, body=%wide.region_4.5_spmd.sunk | while | flops 5 | bytes 115 | solution.py:30
  14.0 0.7 dynamic_slice.8
  15.4 0.7 dynamic_slice.8
  34.9 0.7 copy.13
  35.8 0.7 sub.3
  36.5 0.7 fusion.55
  37.2 0.7 fusion.53
  37.9 0.7 fusion.52
  38.6 0.7 fusion.54
  42.3 40.1 %select_select_fusion = (s32[1024]{0:T(1024)S(1)}, pred[1024]{0:T(1024)(128)(4,1)S(1)}, pred[1024]{0:T(1024)(128)(4,1)S(1)}, pred[1024]{0:T(1024)(128)(4,1)S(1)}...) fusion(s32[]{:T(128)} %bitcast.73, s32[]{:T(128)} %bitcast.74, ...), kind=kLoop, calls=%fused_computation.53 | loop fusion | flops 129024 | bytes 72960 | tf_op jit(solution)/shard_map/gather | solution.py:71
  82.5 40.0 %select_select_fusion.1 = s32[1024]{0:T(1024)S(1)} fusion(pred[1024]{0:T(1024)(128)(4,1)S(1)} %get-tuple-element.165, pred[1024]{0:T(1024)(128)(4,1)S(1)} %get-tuple-element.164, pred[1024]{0:T(1024)(128)(4,1)S(1)} %get-tuple-element.163, pred[1024]{0:T(1024)(128)(4,1)S(1)} %get-tuple-element.162, pred[1024]{0:T(1024)(128)(4,1)S(1)} %get-tuple-element.161, ...), kind=kLoop, calls=%fused_computation.54 | loop fusion | flops 64512 | bytes 68864 | tf_op jit(solution)/shard_map/gather | solution.py:68
  122.5 0.7 fusion.46
  123.2 8.4 %all-to-all-start.1 = ((s32[16,64,1]{1,2,0:T(1,128)}), s32[16,64,1]{1,2,0:T(1,128)S(1)}, u32[]{:S(2)}, u32[]{:S(2)}) async-start(s32[16,64,1]{1,2,0:T(1,128)} %bitcast.137), calls=%async_computation.1 | async-start | bytes 16384 | tf_op jit(solution)/shard_map/all_to_all | solution.py:75
  131.6 1.0 fusion.22
  132.7 2.3 %fusion.23 = bf16[64,1024]{1,0:T(8,128)(2,1)S(1)} fusion(bf16[64,1024]{1,0:T(8,128)(2,1)} %param.8, bf16[1,1024,1024]{2,1,0:T(8,128)(2,1)} %param.9, f32[64]{0:T(128)S(1)} %add_sqrt_fusion.2, f32[1024]{0:T(1024)} %bitcast.161), kind=kOutput, calls=%fused_computation.32 | convolution fusion | flops 134938624 | bytes 2363648 | tf_op jit(solution)/shard_map/while/body/eval_jaxpr/dot_general | solution.py:37
  135.0 3.1 %collective-permute-start = (bf16[64,1024]{1,0:T(8,128)(2,1)S(1)}, bf16[64,1024]{1,0:T(8,128)(2,1)S(1)}, u32[]{:S(2)}, u32[]{:S(2)}) collective-permute-start(bf16[64,1024]{1,0:T(8,128)(2,1)S(1)} %fusion.23), channel_id=1, source_target_pairs={{0,16},{1,17},{2,18},{3,19},{4,20},{5,21},{6,22},{7,23},{8,24},{9,... | collective-permute-start | bytes 393224 | tf_op jit(solution)/shard_map/while/body/eval_jaxpr/ppermute | solution.py:12
  138.2 2.3 %collective-permute-done = bf16[64,1024]{1,0:T(8,128)(2,1)S(1)} collective-permute-done((bf16[64,1024]{1,0:T(8,128)(2,1)S(1)}, bf16[64,1024]{1,0:T(8,128)(2,1)S(1)}, u32[]{:S(2)}, u32[]{:S(2)}) %collective-permute-start) | collective-permute-done | bytes 131104 | tf_op jit(solution)/shard_map/while/body/eval_jaxpr/ppermute | solution.py:12
  140.7 2.2 fusion.30
  142.9 5.2 %all-gather = bf16[128,1024]{1,0:T(8,128)(2,1)S(1)} all-gather(bf16[64,1024]{1,0:T(8,128)(2,1)S(1)} %fusion.30), channel_id=2, replica_groups=mesh['phase'=2,'seq'=16] {'phase'}, dimensions={0}, use_global_device_ids=true | all-gather | bytes 393216 | tf_op jit(solution)/shard_map/all_gather | solution.py:17
  148.2 5.4 %gather_fusion = bf16[1024,1024]{1,0:T(8,128)(2,1)} fusion(bf16[64,1024]{1,0:T(8,128)(2,1)S(1)} %reduce_sum.60, s32[1024]{0:T(1024)S(1)} %broadcast_clamp_fusion), kind=kCustom, calls=%fused_computation | custom fusion | bytes 4198400 | tf_op jit(solution)/shard_map/gather | solution.py:69
  153.6 7.8 %all-to-all-start = ((s32[16,64,1]{1,2,0:T(1,128)}), s32[16,64,1]{1,2,0:T(1,128)S(1)}, u32[]{:S(2)}, u32[]{:S(2)}) async-start(s32[16,64,1]{1,2,0:T(1,128)} %bitcast.72), calls=%async_computation | async-start | bytes 16384 | tf_op jit(solution)/shard_map/all_to_all | solution.py:74
  161.4 3.2 %broadcast_select_fusion = bf16[16,64,1024]{2,1,0:T(8,128)(2,1)} fusion(bf16[16,64,1024]{2,1,0:T(8,128)(2,1)} %bitcast.156, pred[16,64]{1,0:T(8,128)(4,1)S(1)} %fusion.44), kind=kLoop, calls=%fused_computation.5 | loop fusion | flops 1048576 | bytes 4195328 | tf_op jit(solution)/shard_map/jit(_where)/select_n | solution.py:69
  165.1 6.9 %all-to-all-start.2 = ((bf16[16,64,1024]{2,1,0:T(8,128)(2,1)}), bf16[16,64,1024]{2,1,0:T(8,128)(2,1)}, u32[]{:S(2)}, u32[]{:S(2)}) async-start(bf16[16,64,1024]{2,1,0:T(8,128)(2,1)} %broadcast_select_fusion), calls=%async_computation.2 | async-start | bytes 4194304 | tf_op jit(solution)/shard_map/all_to_all | solution.py:73
  172.5 0.7 reduce.8
  173.3 0.7 reduce.9
  174.0 45.5 %all-to-all-done.2 = bf16[16,64,1024]{2,1,0:T(8,128)(2,1)} async-done(((bf16[16,64,1024]{2,1,0:T(8,128)(2,1)}), bf16[16,64,1024]{2,1,0:T(8,128)(2,1)}, u32[]{:S(2)}, u32[]{:S(2)}) %all-to-all-start.2) | async-done | bytes 2097184 | tf_op jit(solution)/shard_map/all_to_all | solution.py:73
  219.6 2.4 %fusion.6 = (f32[256]{0:T(256)S(1)}, bf16[256,1024]{1,0:T(8,128)(2,1)S(1)}) fusion(bf16[1024,1024]{1,0:T(8,128)(2,1)} %bitcast.139, s32[1024]{0:T(1024)S(1)} %lt.87, s32[1024]{0:T(1024)S(1)} %ge.16, s32[256]{0:T(256)S(1)} %iota_add_fusion.1), kind=kOutput, calls=%fused_computation.12 | convolution fusion | flops 538705664 | bytes 2631680 | tf_op jit(solution)/shard_map/dot_general | solution.py:78
  222.0 1.7 fusion.7
  (50 shorter events, 14.2 us)
Async XLA Ops:
  0.6 221.4 %copy-start = (bf16[1024,1024]{1,0:T(8,128)(2,1)S(1)}, bf16[1024,1024]{1,0:T(8,128)(2,1)}, u32[]{:S(2)}) copy-start(bf16[1024,1024]{1,0:T(8,128)(2,1)} %param.11) | copy-start | bytes 6291460
  82.5 58.2 %copy-start.2 = (f32[1,1024]{1,0:T(1,128)S(1)}, f32[1,1024]{1,0:T(1,128)}, u32[]{:S(2)}) copy-start(f32[1,1024]{1,0:T(1,128)} %param.10) | copy-start | bytes 12292
  123.2 30.4 %all-to-all-start.1 = ((s32[16,64,1]{1,2,0:T(1,128)}), s32[16,64,1]{1,2,0:T(1,128)S(1)}, u32[]{:S(2)}, u32[]{:S(2)}) async-start(s32[16,64,1]{1,2,0:T(1,128)} %bitcast.137), calls=%async_computation.1 | async-start | bytes 16384 | tf_op jit(solution)/shard_map/all_to_all | solution.py:75
  135.0 5.6 %collective-permute-start = (bf16[64,1024]{1,0:T(8,128)(2,1)S(1)}, bf16[64,1024]{1,0:T(8,128)(2,1)S(1)}, u32[]{:S(2)}, u32[]{:S(2)}) collective-permute-start(bf16[64,1024]{1,0:T(8,128)(2,1)S(1)} %fusion.23), channel_id=1, source_target_pairs={{0,16},{1,17},{2,18},{3,19},{4,20},{5,21},{6,22},{7,23},{8,24},{9,... | collective-permute-start | bytes 393224 | tf_op jit(solution)/shard_map/while/body/eval_jaxpr/ppermute | solution.py:12
  148.2 5.4 %copy-start.1 = (bf16[64,1024]{1,0:T(8,128)(2,1)}, bf16[64,1024]{1,0:T(8,128)(2,1)S(1)}, u32[]{:S(2)}) copy-start(bf16[64,1024]{1,0:T(8,128)(2,1)S(1)} %reduce_sum.60) | copy-start | bytes 393220
  153.6 11.5 %all-to-all-start = ((s32[16,64,1]{1,2,0:T(1,128)}), s32[16,64,1]{1,2,0:T(1,128)S(1)}, u32[]{:S(2)}, u32[]{:S(2)}) async-start(s32[16,64,1]{1,2,0:T(1,128)} %bitcast.72), calls=%async_computation | async-start | bytes 16384 | tf_op jit(solution)/shard_map/all_to_all | solution.py:74
  165.1 54.4 %all-to-all-start.2 = ((bf16[16,64,1024]{2,1,0:T(8,128)(2,1)}), bf16[16,64,1024]{2,1,0:T(8,128)(2,1)}, u32[]{:S(2)}, u32[]{:S(2)}) async-start(bf16[16,64,1024]{2,1,0:T(8,128)(2,1)} %broadcast_select_fusion), calls=%async_computation.2 | async-start | bytes 4194304 | tf_op jit(solution)/shard_map/all_to_all | solution.py:73
  172.5 49.5 %copy-start.3 = (f32[1024]{0:T(1024)S(1)}, f32[1024]{0:T(1024)}, u32[]{:S(2)}) copy-start(f32[1024]{0:T(1024)} %param.12) | copy-start | bytes 12292
